TPU v7x, 32 devices: a whole 2x2x4 slice. The times are simulated.
32 devices in a mesh: groups: 2 (over x), adapter: 16 (over z, y, core).
Axes of the slice: x: 2, y: 2, z: 4, core: 2. Of those that a mesh axis runs over, the one named last changes fastest.
Arguments:
- tokens: bfloat16 [8192, 8192], P(('groups', 'adapter')), parts along dimension 0, may hold values from -6 to 6
- down_weight: bfloat16 [8192, 2048], P(None, 'adapter'), may hold values from -0.0625 to 0.0625
- up_weight: bfloat16 [2048, 8192], P('adapter'), may hold values from -0.75 to 0.75
- slot_adapter_index: int32 [992], P(('groups', 'adapter')), parts along dimension 0, may hold values from 0 to 31, as said below
- slot_token_length: int32 [992], P(('groups', 'adapter')), parts along dimension 0, may hold values from 0 to 48, as said below
- adapter_block_table: int32 [64], P('groups'), parts along dimension 0, may hold values from 0 to 31, as said below
Outputs:
- projection_update: bfloat16 [8192, 8192], P(('groups', 'adapter')), parts along dimension 0
There are 2 independent parts, one for each index of `groups`. A program takes and returns all parts, laid end to end along the dimension named above; an argument that names none is the same for every part. Nothing has to cross between parts.
Inputs may be any that keep to these rules, and one draw needn't show every extreme that they name: `adapter_block_table`: A permutation: block b is stored on device b // 2 of the adapter axis. `slot_adapter_index`: slot 0 of every device uses one and the same adapter. Apart from slot 0, the slots of one device put at most 24 tokens on the adapters stored on any one device, none on the device that stores slot 0's adapter, and exactly 24 on some device. `slot_token_length`: the 31 lengths of one device sum to 256; slot 0 of each device has 48 tokens; other slots may be empty.
All inputs are finite; a program needn't handle non-finite values.
Results may differ from a plain program's by a relative error of at most 0.0051.
Values may be sent and summed in bfloat16 or wider, within the bound.
A program may use at most 128 MiB of HBM per device.

v0:
```python
import jax
import jax.numpy as jnp
from jax import lax
from jax.sharding import PartitionSpec as P

ADAPTER_RANK = 64


def route(slot_adapter_index, slot_token_length, adapter_block_table, tok_count, hot_rows):
    catalog = jnp.arange(adapter_block_table.shape[0], dtype=jnp.int32)
    position = jnp.sum(
        jnp.where(slot_adapter_index[:, None] == catalog[None, :], adapter_block_table[None, :], 0),
        axis=1,
    )
    span_ends = jnp.cumsum(slot_token_length)
    span_starts = span_ends - slot_token_length
    token_index = jnp.arange(hot_rows, tok_count, dtype=jnp.int32)
    inside = (token_index[:, None] >= span_starts[None, :]) & (
        token_index[:, None] < span_ends[None, :]
    )
    block = jnp.sum(jnp.where(inside, position[None, :], 0), axis=1)
    return position[0], block


def rank_among(owner):
    index = jnp.arange(owner.shape[0], dtype=jnp.int32)
    earlier = (owner[None, :] == owner[:, None]) & (index[None, :] < index[:, None])
    return jnp.sum(earlier.astype(jnp.int32), axis=1)


def hot_weights(hot_block, down_weight, up_weight, loaded_block):
    mine = hot_block // loaded_block == lax.axis_index("adapter")
    start = (hot_block % loaded_block) * ADAPTER_RANK
    down = lax.dynamic_slice_in_dim(down_weight, start, ADAPTER_RANK, 1)
    up = lax.dynamic_slice_in_dim(up_weight, start, ADAPTER_RANK, 0)
    down = lax.psum(jnp.where(mine, down, 0), "adapter")
    up = lax.psum(jnp.where(mine, up, 0), "adapter")
    return down, up


def apply_pair(rows, down, up):
    shrink = jnp.dot(rows, down, preferred_element_type=jnp.float32).astype(jnp.bfloat16)
    return jnp.dot(shrink, up, preferred_element_type=jnp.float32).astype(jnp.bfloat16)


def on_device(
    tokens, down_weight, up_weight, slot_adapter_index, slot_token_length, adapter_block_table
):
    devices = lax.axis_size("adapter")
    tok_count, width = tokens.shape
    hot_rows = 3 * tok_count // devices
    cap = hot_rows // 2
    loaded_block = down_weight.shape[1] // ADAPTER_RANK
    hot_block, block = route(
        slot_adapter_index, slot_token_length, adapter_block_table, tok_count, hot_rows
    )
    hot_down, hot_up = hot_weights(hot_block, down_weight, up_weight, loaded_block)
    cold = tokens[hot_rows:]
    owner = block // loaded_block
    slot_of_token = owner * cap + rank_among(owner)
    slot_index = jnp.arange(devices * cap, dtype=jnp.int32)
    hit = slot_index[:, None] == slot_of_token[None, :]
    pick = hit.astype(jnp.bfloat16)
    outgoing = jnp.dot(pick, cold, preferred_element_type=jnp.float32).astype(jnp.bfloat16)
    outgoing = outgoing.reshape(devices, cap, width)
    slot_tags = jnp.sum(jnp.where(hit, (block % loaded_block)[None, :], 0), axis=1)
    slot_tags = slot_tags.astype(jnp.bfloat16).reshape(devices, cap)
    incoming = lax.all_to_all(outgoing, "adapter", split_axis=0, concat_axis=0, tiled=True)
    tags = lax.all_to_all(slot_tags, "adapter", split_axis=0, concat_axis=0, tiled=True)
    rows = incoming.reshape(devices * cap, width)
    shrink = jnp.dot(rows, down_weight, preferred_element_type=jnp.float32)
    column_slot = jnp.arange(loaded_block * ADAPTER_RANK, dtype=jnp.int32) // ADAPTER_RANK
    keep = tags.reshape(-1).astype(jnp.int32)[:, None] == column_slot[None, :]
    shrink = jnp.where(keep, shrink, 0.0).astype(jnp.bfloat16)
    update = jnp.dot(shrink, up_weight, preferred_element_type=jnp.float32).astype(jnp.bfloat16)
    update = update.reshape(devices, cap, width)
    returned = lax.all_to_all(update, "adapter", split_axis=0, concat_axis=0, tiled=True)
    returned = returned.reshape(devices * cap, width)
    cold_update = jnp.dot(pick.T, returned, preferred_element_type=jnp.float32)
    hot_update = apply_pair(tokens[:hot_rows], hot_down, hot_up)
    return jnp.concatenate([hot_update, cold_update.astype(jnp.bfloat16)], axis=0)


def solution(mesh):
    in_specs = (
        P(("groups", "adapter"), None),
        P(None, "adapter"),
        P("adapter", None),
        P(("groups", "adapter")),
        P(("groups", "adapter")),
        P("groups"),
    )
    out_specs = P(("groups", "adapter"), None)
    return jax.shard_map(
        on_device, mesh=mesh, in_specs=in_specs, out_specs=out_specs, check_vma=False
    )
```

profile of v0, /device:TPU:1, one launch (start us, length us, event | category | flops | bytes accessed | tf_op | source)
XLA Modules:
  0.0 416.2 jit_solution(8469112706409810991)
XLA Ops:
  6.5 0.7 copy.11
  7.3 0.1 reduce-window.8
  7.3 0.1 reduce
  7.5 0.7 sub.20
  8.1 0.8 select_reduce_fusion.2
  9.0 0.1 select_reduce_fusion.1
  9.1 0.2 convert_reduce_fusion
  9.3 0.1 select_reduce_fusion
  9.4 0.7 convert_element_type.63
  10.1 7.3 %all-to-all-start = ((bf16[16,1,24]{2,1,0:T(2,128)(2,1)}), bf16[16,1,24]{2,1,0:T(2,128)(2,1)S(1)}, u32[]{:S(2)}, u32[]{:S(2)}) async-start(bf16[16,1,24]{2,1,0:T(2,128)(2,1)} %convert_element_type.63), calls=%async_computation | async-start | bytes 16384 | tf_op jit(solution)/shard_map/all_to_all | solution.py:69
  17.5 6.5 %convolution_convert_fusion.1 = bf16[384,8192]{1,0:T(8,128)(2,1)} fusion(bf16[256,8192]{1,0:T(8,128)(2,1)} %param.6, s32[208]{0:T(256)S(1)} %multiply_add_fusion), kind=kOutput, calls=%fused_computation.1 | convolution fusion | flops 1311848448 | bytes 9700160 | tf_op jit(solution)/shard_map/dot_general | solution.py:64
  24.0 0.0 all-to-all-done
  24.0 0.0 copy-start
  24.0 6.1 %all-to-all-start.1 = ((bf16[16,24,8192]{2,1,0:T(8,128)(2,1)}), bf16[16,24,8192]{2,1,0:T(8,128)(2,1)}, u32[]{:S(2)}, u32[]{:S(2)}) async-start(bf16[16,24,8192]{2,1,0:T(8,128)(2,1)} %bitcast.13), calls=%async_computation.1 | async-start | bytes 12582912 | tf_op jit(solution)/shard_map/all_to_all | solution.py:68
  30.2 0.1 reshape.139
  30.3 114.5 %all-to-all-done.1 = bf16[16,24,8192]{2,1,0:T(8,128)(2,1)} async-done(((bf16[16,24,8192]{2,1,0:T(8,128)(2,1)}), bf16[16,24,8192]{2,1,0:T(8,128)(2,1)}, u32[]{:S(2)}, u32[]{:S(2)}) %all-to-all-start.1) | async-done | bytes 6291488 | tf_op jit(solution)/shard_map/all_to_all | solution.py:68
  144.8 0.0 copy-done
  144.8 12.7 %convolution_convert_fusion = bf16[384,8192]{1,0:T(8,128)(2,1)} fusion(bf16[128,8192]{1,0:T(8,128)(2,1)} %param.8, bf16[384,8192]{1,0:T(8,128)(2,1)} %bitcast.3, bf16[8192,128]{1,0:T(8,128)(2,1)S(1)} %copy-done, s32[128]{0:T(128)S(1)} %and_select_fusion, s32[384]{0:T(512)S(1)} %reshape.139), kind=kOutput, calls=%fused_computation | convolution fusion | flops 1613905920 | bytes 16779264 | tf_op jit(solution)/shard_map/dot_general | solution.py:75
  157.5 27.7 %all-to-all-start.2 = ((bf16[16,24,8192]{2,1,0:T(8,128)(2,1)}), bf16[16,24,8192]{2,1,0:T(8,128)(2,1)}, u32[]{:S(2)}, u32[]{:S(2)}) async-start(bf16[16,24,8192]{2,1,0:T(8,128)(2,1)} %bitcast.14), calls=%async_computation.2 | async-start | bytes 12582912 | tf_op jit(solution)/shard_map/all_to_all | solution.py:77
  185.2 0.0 all-reduce.3.cloned.1.call-start
  185.5 2.4 dynamic-slice_select_fusion.1
  187.9 2.1 dynamic-slice_select_fusion
  190.0 0.0 all-reduce.3.cloned.1.call-update
  190.0 209.3 %all-reduce.3.cloned.1.call-done = (bf16[64,8192]{1,0:T(8,128)(2,1)}, bf16[8192,64]{1,0:T(8,128)(2,1)}) async-done(((bf16[64,8192]{1,0:T(8,128)(2,1)}, bf16[8192,64]{1,0:T(8,128)(2,1)}), (bf16[64,8192]{1,0:T(8,128)(2,1)}, bf16[8192,64]{1,0:T(8,128)(2,1)})) %all-reduce.3.cloned.1.call-update) | async-done | bytes 2097168 | tf_op jit(solution)/shard_map/psum | solution.py:37
  399.3 2.9 convolution_convert_fusion.3
  402.2 0.0 all-to-all-done.2
  402.2 4.8 %convolution_convert_fusion.2 = bf16[208,8192]{1,0:T(8,128)(2,1)S(1)} fusion(bf16[384,8192]{1,0:T(8,128)(2,1)} %bitcast.5, s32[208]{0:T(256)S(1)} %multiply_add_fusion), kind=kOutput, calls=%fused_computation.2 | convolution fusion | flops 1310406656 | bytes 9700160 | tf_op jit(solution)/shard_map/dot_general | solution.py:79
  406.9 2.5 pad_maximum_fusion
  (6 shorter events, 0.1 us)
Async XLA Ops:
  10.1 13.9 %all-to-all-start = ((bf16[16,1,24]{2,1,0:T(2,128)(2,1)}), bf16[16,1,24]{2,1,0:T(2,128)(2,1)S(1)}, u32[]{:S(2)}, u32[]{:S(2)}) async-start(bf16[16,1,24]{2,1,0:T(2,128)(2,1)} %convert_element_type.63), calls=%async_computation | async-start | bytes 16384 | tf_op jit(solution)/shard_map/all_to_all | solution.py:69
  24.0 120.8 %copy-start = (bf16[8192,128]{1,0:T(8,128)(2,1)S(1)}, bf16[8192,128]{1,0:T(8,128)(2,1)}, u32[]{:S(2)}) copy-start(bf16[8192,128]{1,0:T(8,128)(2,1)} %param.7) | copy-start | bytes 6291460
  24.0 120.8 %all-to-all-start.1 = ((bf16[16,24,8192]{2,1,0:T(8,128)(2,1)}), bf16[16,24,8192]{2,1,0:T(8,128)(2,1)}, u32[]{:S(2)}, u32[]{:S(2)}) async-start(bf16[16,24,8192]{2,1,0:T(8,128)(2,1)} %bitcast.13), calls=%async_computation.1 | async-start | bytes 12582912 | tf_op jit(solution)/shard_map/all_to_all | solution.py:68
  157.5 244.6 %all-to-all-start.2 = ((bf16[16,24,8192]{2,1,0:T(8,128)(2,1)}), bf16[16,24,8192]{2,1,0:T(8,128)(2,1)}, u32[]{:S(2)}, u32[]{:S(2)}) async-start(bf16[16,24,8192]{2,1,0:T(8,128)(2,1)} %bitcast.14), calls=%async_computation.2 | async-start | bytes 12582912 | tf_op jit(solution)/shard_map/all_to_all | solution.py:77
  185.2 214.0 %all-reduce.3.cloned.1.call-start = ((), (), s32[]{:S(2)}) async-start(), calls=%async_computation.3 | async-start | bytes 6291456 | tf_op jit(solution)/shard_map/psum | solution.py:37
Sparse Core Ops, SparseCore 0:
  190.1 209.1 all-reduce.2
where the time goes:
time: 419 us; the launch traced here: 416 us
  waiting for transfers between devices  324 us (77%)
  starting transfers between devices  41.2 us (10%)
  matrix products  26.9 us (6%)
  between operations  13.6 us (3%)
  other arithmetic  9.11 us (2%)
    psum x1, waiting for transfers between devices, hot_weights(): up = lax.psum(jnp.where(mine, up, 0), 'adapter')  209 us
    all_to_all x1, waiting for transfers between devices, on_device(): lax.all_to_all(outgoing, 'adapter', split_axis=0, concat_axis=0, tiled=True)  114 us
    all_to_all x1, starting transfers between devices, on_device(): lax.all_to_all(update, 'adapter', split_axis=0, concat_axis=0, tiled=True)  27.7 us
    dot_general x1, matrix products, on_device(): jnp.dot(shrink, up_weight, preferred_element_type=jnp.float32)  12.7 us
  transfers between devices with their start and end apart: 4, of which 2 were waited for; matrix products, arithmetic and copies ran while one was open for 3% of the time, Pallas kernels for 0%

commit v1 on v0

--- a/solution.py
+++ b/solution.py
@@ -1,6 +1,8 @@
 import jax
 import jax.numpy as jnp
 from jax import lax
+from jax.experimental import pallas as pl
+from jax.experimental.pallas import tpu as pltpu
 from jax.sharding import PartitionSpec as P
 
 ADAPTER_RANK = 64
@@ -43,7 +45,7 @@
     return jnp.dot(shrink, up, preferred_element_type=jnp.float32).astype(jnp.bfloat16)
 
 
-def on_device(
+def exchange_all(
     tokens, down_weight, up_weight, slot_adapter_index, slot_token_length, adapter_block_table
 ):
     devices = lax.axis_size("adapter")
@@ -81,7 +83,310 @@
     return jnp.concatenate([hot_update, cold_update.astype(jnp.bfloat16)], axis=0)
 
 
+PLANE = 4
+LINE = 4
+MESH = pl.DeviceIdType.MESH
+
+
+def plane_kernel(
+    cap, out_ref, tag_ref, down_ref, up_ref, ret_ref,
+    rows, tags, down, up, result,
+    local_sem, tok_send, tok_recv, tag_send, tag_recv,
+    right_send, left_send, x_send, z_recv, x_recv, ret_send, ret_recv, own_sem,
+):
+    group = lax.axis_index("groups")
+    me = lax.axis_index("adapter")
+    z = me // PLANE
+    q = me % PLANE
+    other = 1 - group
+    width = rows.shape[2]
+    half_down = down.shape[1] // 2
+    half_up = up.shape[1] // 2
+
+    def peer(e):
+        return (q + e) % PLANE
+
+    own = [
+        pltpu.make_async_copy(down_ref, down.at[z], local_sem.at[0]),
+        pltpu.make_async_copy(up_ref, up.at[z], local_sem.at[1]),
+        pltpu.make_async_copy(out_ref.at[q], rows.at[q], local_sem.at[2]),
+        pltpu.make_async_copy(tag_ref.at[q], tags.at[q], local_sem.at[3]),
+    ]
+    for copy in own:
+        copy.start()
+
+    barrier = pltpu.get_barrier_semaphore()
+    for e in range(1, PLANE):
+        pl.semaphore_signal(
+            barrier, inc=1, device_id=(group, z * PLANE + peer(e)), device_id_type=MESH
+        )
+    pl.semaphore_signal(barrier, inc=1, device_id=(other, me), device_id_type=MESH)
+
+    @pl.when(z > 0)
+    def _():
+        pl.semaphore_signal(barrier, inc=1, device_id=(group, me - PLANE), device_id_type=MESH)
+
+    @pl.when(z < LINE - 1)
+    def _():
+        pl.semaphore_signal(barrier, inc=1, device_id=(group, me + PLANE), device_id_type=MESH)
+
+    pl.semaphore_wait(barrier, PLANE + 1 + (z % (LINE - 1) + LINE - 2) // (LINE - 1))
+
+    for copy in own[:2]:
+        copy.wait()
+
+    def part(kind, origin, half):
+        if kind == 0:
+            return down.at[origin, pl.ds(pl.multiple_of(half * half_down, 128), half_down), :]
+        return up.at[origin, pl.ds(pl.multiple_of(half * half_up, 16), half_up), :]
+
+    def remote(kind, origin, half, send, recv, device):
+        ref = part(kind, origin, half)
+        return pltpu.make_async_remote_copy(
+            src_ref=ref, dst_ref=ref,
+            send_sem=send.at[origin, kind], recv_sem=recv.at[origin, kind],
+            device_id=device, device_id_type=MESH,
+        )
+
+    def to_right(kind, origin):
+        return remote(kind, origin, group, right_send, z_recv, (group, me + PLANE))
+
+    def to_left(kind, origin):
+        return remote(kind, origin, group, left_send, z_recv, (group, me - PLANE))
+
+    def to_other(kind, origin):
+        return remote(kind, origin, group, x_send, x_recv, (other, me))
+
+    def from_other(kind, origin):
+        return remote(kind, origin, other, x_send, x_recv, (other, me))
+
+    for kind in range(2):
+        @pl.when(z < LINE - 1)
+        def _():
+            to_right(kind, z).start()
+
+        @pl.when(z > 0)
+        def _():
+            to_left(kind, z).start()
+
+    def token_copy(e, slot):
+        return pltpu.make_async_remote_copy(
+            src_ref=out_ref.at[peer(e)], dst_ref=rows.at[slot],
+            send_sem=tok_send.at[e], recv_sem=tok_recv.at[e],
+            device_id=(group, z * PLANE + peer(e)), device_id_type=MESH,
+        )
+
+    def tag_copy(e, slot):
+        return pltpu.make_async_remote_copy(
+            src_ref=tag_ref.at[peer(e)], dst_ref=tags.at[slot],
+            send_sem=tag_send.at[e], recv_sem=tag_recv.at[e],
+            device_id=(group, z * PLANE + peer(e)), device_id_type=MESH,
+        )
+
+    for e in range(1, PLANE):
+        tag_copy(e, q).start()
+        token_copy(e, q).start()
+
+    def pass_on(d):
+        for kind in range(2):
+            @pl.when(z >= d)
+            def _():
+                origin = z - d
+                to_right_like = remote(kind, origin, group, right_send, z_recv, (other, me))
+                to_right_like.wait_recv()
+                to_other(kind, origin).start()
+
+                @pl.when(z < LINE - 1)
+                def _():
+                    to_right(kind, origin).start()
+
+            @pl.when(z + d < LINE)
+            def _():
+                origin = z + d
+                to_left_like = remote(kind, origin, group, left_send, z_recv, (other, me))
+                to_left_like.wait_recv()
+                to_other(kind, origin).start()
+
+                @pl.when(z > 0)
+                def _():
+                    to_left(kind, origin).start()
+
+    def back(phase, first, count, e, slot):
+        return pltpu.make_async_remote_copy(
+            src_ref=result.at[peer(e), pl.ds(first, count), :],
+            dst_ref=ret_ref.at[slot, pl.ds(first, count), :],
+            send_sem=ret_send.at[phase, e], recv_sem=ret_recv.at[phase, e],
+            device_id=(group, z * PLANE + peer(e)), device_id_type=MESH,
+        )
+
+    def keep_own(phase, first, count):
+        return pltpu.make_async_copy(
+            result.at[q, pl.ds(first, count), :],
+            ret_ref.at[q, pl.ds(first, count), :],
+            own_sem.at[phase],
+        )
+
+    def compute(phase, first, count, origins):
+        step = 1024
+
+        def shrink_step(t, sums):
+            k = pl.ds(pl.multiple_of(t * step, step), step)
+            x = rows[:, first : first + count, k].reshape(PLANE * count, step)
+            return tuple(
+                s + jnp.dot(x, down[o, k, :], preferred_element_type=jnp.float32)
+                for s, o in zip(sums, origins)
+            )
+
+        lanes = down.shape[2]
+        zero = jnp.zeros((PLANE * count, lanes), jnp.float32)
+        sums = lax.fori_loop(0, width // step, shrink_step, tuple(zero for _ in origins))
+        tag = tags[:, first : first + count, :].reshape(PLANE * count, lanes).astype(jnp.float32)
+        slot = lax.broadcasted_iota(jnp.int32, (PLANE * count, lanes), 1) // ADAPTER_RANK
+        tag = tag.astype(jnp.int32) - slot
+        loaded = lanes // ADAPTER_RANK
+        masked = [
+            jnp.where(tag == o * loaded, s, 0.0).astype(jnp.bfloat16)
+            for s, o in zip(sums, origins)
+        ]
+        tile = 512
+
+        def up_step(t, carry):
+            c = pl.ds(pl.multiple_of(t * tile, tile), tile)
+            total = jnp.zeros((PLANE * count, tile), jnp.float32)
+            for m, o in zip(masked, origins):
+                total += jnp.dot(m, up[o, :, c], preferred_element_type=jnp.float32)
+            result[:, first : first + count, c] = total.astype(jnp.bfloat16).reshape(
+                PLANE, count, tile
+            )
+            return carry
+
+        lax.fori_loop(0, width // tile, up_step, 0)
+        for e in range(1, PLANE):
+            back(phase, first, count, e, q).start()
+        keep_own(phase, first, count).start()
+
+    def arrive(origin):
+        for kind in range(2):
+            from_other(kind, origin).wait_recv()
+
+    near = z + 1 - 2 * (z % 2)
+    third = 2 - z // 2
+    far = 3 * (1 - z // 2)
+    phases = ((0, 2 * cap), (2 * cap, cap + 8), (3 * cap + 8, 2 * cap))
+
+    pass_on(1)
+    pass_on(2)
+    for copy in own[2:]:
+        copy.wait()
+    for e in range(1, PLANE):
+        tag_copy(e, (q + PLANE - e) % PLANE).wait_recv()
+        token_copy(e, (q + PLANE - e) % PLANE).wait_recv()
+    arrive(near)
+    compute(0, *phases[0], (z, near))
+    pass_on(3)
+    arrive(third)
+    compute(1, *phases[1], (third,))
+    arrive(far)
+    compute(2, *phases[2], (z, near, third, far))
+
+    for e in range(1, PLANE):
+        tag_copy(e, q).wait_send()
+        token_copy(e, q).wait_send()
+    for kind in range(2):
+        for d in range(LINE):
+            @pl.when((z >= d) & (z < LINE - 1))
+            def _():
+                to_right(kind, z - d).wait_send()
+
+            @pl.when((z + d < LINE) & (z > 0))
+            def _():
+                to_left(kind, z + d).wait_send()
+
+        for origin in (near, third, far):
+            to_other(kind, origin).wait_send()
+    for phase, (first, count) in enumerate(phases):
+        keep_own(phase, first, count).wait()
+        for e in range(1, PLANE):
+            back(phase, first, count, e, q).wait_send()
+            back(phase, first, count, e, (q + PLANE - e) % PLANE).wait_recv()
+
+
+def exchange_planes(
+    tokens, down_weight, up_weight, slot_adapter_index, slot_token_length, adapter_block_table
+):
+    devices = lax.axis_size("adapter")
+    tok_count, width = tokens.shape
+    cap = 3 * tok_count // devices // 2
+    lanes = down_weight.shape[1]
+    loaded_block = lanes // ADAPTER_RANK
+    me = lax.axis_index("adapter")
+    z = me // PLANE
+    _, block = route(slot_adapter_index, slot_token_length, adapter_block_table, tok_count, 0)
+    owner = block // loaded_block
+    rank = rank_among(owner)
+    origin = owner // PLANE
+    near = z + 1 - 2 * (z % 2)
+    third = 2 - z // 2
+    base = jnp.where(
+        origin == z,
+        0,
+        jnp.where(origin == near, cap, jnp.where(origin == third, 2 * cap, 3 * cap + 8)),
+    )
+    base = jnp.where(rank < cap, base, 3 * cap + 8)
+    slots = 5 * cap + 8
+    slot_of_token = (owner % PLANE) * slots + base + rank
+    slot_index = jnp.arange(PLANE * slots, dtype=jnp.int32)
+    hit = slot_index[:, None] == slot_of_token[None, :]
+    pick = hit.astype(jnp.bfloat16)
+    outgoing = jnp.dot(pick, tokens, preferred_element_type=jnp.float32).astype(jnp.bfloat16)
+    outgoing = outgoing.reshape(PLANE, slots, width)
+    tag = jnp.sum(jnp.where(hit, (origin * loaded_block + block % loaded_block)[None, :], 0), axis=1)
+    tag = jnp.broadcast_to(tag.astype(jnp.bfloat16)[:, None], (PLANE * slots, lanes))
+    tag = tag.reshape(PLANE, slots, lanes)
+    dma = pltpu.SemaphoreType.DMA
+    returned = pl.pallas_call(
+        lambda *refs: plane_kernel(cap, *refs),
+        out_shape=jax.ShapeDtypeStruct((PLANE, slots, width), jnp.bfloat16),
+        in_specs=[pl.BlockSpec(memory_space=pl.ANY)] * 4,
+        out_specs=pl.BlockSpec(memory_space=pl.ANY),
+        scratch_shapes=[
+            pltpu.VMEM((PLANE, slots, width), jnp.bfloat16),
+            pltpu.VMEM((PLANE, slots, lanes), jnp.bfloat16),
+            pltpu.VMEM((LINE, width, lanes), jnp.bfloat16),
+            pltpu.VMEM((LINE, lanes, width), jnp.bfloat16),
+            pltpu.VMEM((PLANE, slots, width), jnp.bfloat16),
+            dma((4,)),
+            dma((PLANE,)),
+            dma((PLANE,)),
+            dma((PLANE,)),
+            dma((PLANE,)),
+            dma((LINE, 2)),
+            dma((LINE, 2)),
+            dma((LINE, 2)),
+            dma((LINE, 2)),
+            dma((LINE, 2)),
+            dma((3, PLANE)),
+            dma((3, PLANE)),
+            dma((3,)),
+        ],
+        compiler_params=pltpu.CompilerParams(
+            collective_id=0, has_side_effects=True, vmem_limit_bytes=56 * 2**20
+        ),
+        cost_estimate=pl.CostEstimate(
+            flops=8 * PLANE * slots * width * lanes,
+            bytes_accessed=8 * PLANE * slots * width,
+            transcendentals=0,
+        ),
+    )(outgoing, tag, down_weight, up_weight)
+    returned = returned.reshape(PLANE * slots, width)
+    update = jnp.dot(pick.T, returned, preferred_element_type=jnp.float32)
+    return update.astype(jnp.bfloat16)
+
+
 def solution(mesh):
+    sizes = dict(mesh.shape)
+    planes = sizes["groups"] == 2 and sizes["adapter"] == PLANE * LINE
+    on_device = exchange_planes if planes else exchange_all
     in_specs = (
         P(("groups", "adapter"), None),
         P(None, "adapter"),

time: 419 us -> 235 us (0.56)
  the two profiles are of different devices: /device:TPU:1 before, /device:TPU:17 now
where the time goes in v1:
time: 235 us; the launch traced here: 234 us
  Pallas kernels  215 us (91%)
  matrix products  15.5 us (7%)
    pallas_call x1, Pallas kernels, exchange_planes(): pl.pallas_call(lambda *refs: plane_kernel(cap, *refs), out_shape=jax.Shap...  215 us
    dot_general x1, matrix products, exchange_planes(): update = jnp.dot(pick.T, returned, preferred_element_type=jnp.float32)  7.8 us
    dot_general x1, matrix products, exchange_planes(): jnp.dot(pick, tokens, preferred_element_type=jnp.float32)  7.75 us

profile of v1, /device:TPU:17, one launch (start us, length us, event | category | flops | bytes accessed | tf_op | source)
XLA Modules:
  0.0 234.5 jit_solution(12591103615842364764)
XLA Ops:
  0.0 0.8 select_reduce_fusion.2
  0.9 0.8 copy.9
  1.6 0.1 reduce-window.8
  1.7 0.1 reduce
  1.8 0.7 sub.26
  2.4 0.1 select_reduce_fusion.1
  2.6 0.2 convert_reduce_fusion
  2.8 0.2 select_reduce_fusion
  2.9 0.8 broadcast_in_dim.78.refs_1_
  3.7 7.7 %convolution_convert_fusion = bf16[512,8192]{1,0:T(8,128)(2,1)} fusion(bf16[256,8192]{1,0:T(8,128)(2,1)} %param.6, s32[256]{0:T(256)S(1)} %fusion.6), kind=kOutput, calls=%fused_computation | convolution fusion | flops 2151809024 | bytes 12583936 | tf_op jit(solution)/shard_map/dot_general | solution.py:341
  11.5 215.2 %shard_map.64 = bf16[4,128,8192]{2,1,0:T(8,128)(2,1)} custom-call(bf16[4,128,8192]{2,1,0:T(8,128)(2,1)} %bitcast.7, bf16[4,128,128]{2,1,0:T(8,128)(2,1)} %broadcast_in_dim.78.refs_1_, bf16[8192,128]{1,0:T(8,128)(2,1)} %refs_2_.1, bf16[128,8192]{1,0:T(8,128)(2,1)} %refs_3_.1), custom_call_target="tpu_custom_call" | custom-call | flops 4294967296 | bytes 33554432 | tf_op jit(solution)/shard_map/pallas_call | solution.py:347
  226.7 7.8 %convolution_convert_fusion.1 = bf16[256,8192]{1,0:T(8,128)(2,1)} fusion(bf16[512,8192]{1,0:T(8,128)(2,1)} %bitcast.8, s32[256]{0:T(256)S(1)} %fusion.6), kind=kOutput, calls=%fused_computation.1 | convolution fusion | flops 2149711872 | bytes 12583936 | tf_op jit(solution)/shard_map/dot_general | solution.py:382
  (3 shorter events, 0.0 us)

commit v2 on v1

--- a/solution.py
+++ b/solution.py
@@ -85,12 +85,13 @@
 
 PLANE = 4
 LINE = 4
+DOWN_PARTS = 2
 MESH = pl.DeviceIdType.MESH
 
 
 def plane_kernel(
-    cap, out_ref, tag_ref, down_ref, up_ref, ret_ref,
-    rows, tags, down, up, result,
+    tiles, out_ref, tag_ref, down_ref, up_ref, ret_ref,
+    rows, tags, down, up, result, shrink,
     local_sem, tok_send, tok_recv, tag_send, tag_recv,
     right_send, left_send, x_send, z_recv, x_recv, ret_send, ret_recv, own_sem,
 ):
@@ -100,6 +101,7 @@
     q = me % PLANE
     other = 1 - group
     width = rows.shape[2]
+    kinds = DOWN_PARTS + len(tiles)
     half_down = down.shape[1] // 2
     half_up = up.shape[1] // 2
 
@@ -136,9 +138,13 @@
         copy.wait()
 
     def part(kind, origin, half):
-        if kind == 0:
-            return down.at[origin, pl.ds(pl.multiple_of(half * half_down, 128), half_down), :]
-        return up.at[origin, pl.ds(pl.multiple_of(half * half_up, 16), half_up), :]
+        if kind < DOWN_PARTS:
+            count = half_down // DOWN_PARTS
+            start = half * half_down + kind * count
+            return down.at[origin, pl.ds(pl.multiple_of(start, 128), count), :]
+        first, count = tiles[kind - DOWN_PARTS]
+        lines = pl.ds(pl.multiple_of(half * half_up, 16), half_up)
+        return up.at[origin, lines, pl.ds(first, count)]
 
     def remote(kind, origin, half, send, recv, device):
         ref = part(kind, origin, half)
@@ -160,7 +166,7 @@
     def from_other(kind, origin):
         return remote(kind, origin, other, x_send, x_recv, (other, me))
 
-    for kind in range(2):
+    def send_own(kind):
         @pl.when(z < LINE - 1)
         def _():
             to_right(kind, z).start()
@@ -168,6 +174,9 @@
         @pl.when(z > 0)
         def _():
             to_left(kind, z).start()
+
+    send_own(0)
+    send_own(1)
 
     def token_copy(e, slot):
         return pltpu.make_async_remote_copy(
@@ -187,112 +196,112 @@
         tag_copy(e, q).start()
         token_copy(e, q).start()
 
-    def pass_on(d):
-        for kind in range(2):
+    def pass_on(kind):
+        if kind + 2 < kinds:
+            send_own(kind + 2)
+        for d in range(1, LINE):
             @pl.when(z >= d)
             def _():
                 origin = z - d
-                to_right_like = remote(kind, origin, group, right_send, z_recv, (other, me))
-                to_right_like.wait_recv()
-                to_other(kind, origin).start()
+                remote(kind, origin, group, right_send, z_recv, (other, me)).wait_recv()
 
                 @pl.when(z < LINE - 1)
                 def _():
                     to_right(kind, origin).start()
 
+                to_other(kind, origin).start()
+
             @pl.when(z + d < LINE)
             def _():
                 origin = z + d
-                to_left_like = remote(kind, origin, group, left_send, z_recv, (other, me))
-                to_left_like.wait_recv()
-                to_other(kind, origin).start()
+                remote(kind, origin, group, left_send, z_recv, (other, me)).wait_recv()
 
                 @pl.when(z > 0)
                 def _():
                     to_left(kind, origin).start()
 
-    def back(phase, first, count, e, slot):
+                to_other(kind, origin).start()
+
+    def back(t, e, slot):
+        columns = pl.ds(*tiles[t])
         return pltpu.make_async_remote_copy(
-            src_ref=result.at[peer(e), pl.ds(first, count), :],
-            dst_ref=ret_ref.at[slot, pl.ds(first, count), :],
-            send_sem=ret_send.at[phase, e], recv_sem=ret_recv.at[phase, e],
+            src_ref=result.at[peer(e), :, columns],
+            dst_ref=ret_ref.at[slot, :, columns],
+            send_sem=ret_send.at[t, e], recv_sem=ret_recv.at[t, e],
             device_id=(group, z * PLANE + peer(e)), device_id_type=MESH,
         )
 
-    def keep_own(phase, first, count):
+    def keep_own(t):
+        columns = pl.ds(*tiles[t])
         return pltpu.make_async_copy(
-            result.at[q, pl.ds(first, count), :],
-            ret_ref.at[q, pl.ds(first, count), :],
-            own_sem.at[phase],
-        )
-
-    def compute(phase, first, count, origins):
+            result.at[q, :, columns], ret_ref.at[q, :, columns], own_sem.at[t]
+        )
+
+    slots = rows.shape[1]
+    lanes = down.shape[2]
+    total_rows = PLANE * slots
+    origins = (z, z + 1 - 2 * (z % 2), 2 - z // 2, 3 * (1 - z // 2))
+
+    def arrive(kind):
+        for origin in origins[1:]:
+            from_other(kind, origin).wait_recv()
+
+    def shrink_all():
         step = 1024
-
-        def shrink_step(t, sums):
-            k = pl.ds(pl.multiple_of(t * step, step), step)
-            x = rows[:, first : first + count, k].reshape(PLANE * count, step)
-            return tuple(
-                s + jnp.dot(x, down[o, k, :], preferred_element_type=jnp.float32)
-                for s, o in zip(sums, origins)
-            )
-
-        lanes = down.shape[2]
-        zero = jnp.zeros((PLANE * count, lanes), jnp.float32)
-        sums = lax.fori_loop(0, width // step, shrink_step, tuple(zero for _ in origins))
-        tag = tags[:, first : first + count, :].reshape(PLANE * count, lanes).astype(jnp.float32)
-        slot = lax.broadcasted_iota(jnp.int32, (PLANE * count, lanes), 1) // ADAPTER_RANK
-        tag = tag.astype(jnp.int32) - slot
-        loaded = lanes // ADAPTER_RANK
-        masked = [
-            jnp.where(tag == o * loaded, s, 0.0).astype(jnp.bfloat16)
-            for s, o in zip(sums, origins)
-        ]
+        tag = tags[...].reshape(total_rows, lanes).astype(jnp.int32)
+        tag = tag - lax.broadcasted_iota(jnp.int32, (total_rows, lanes), 1) // ADAPTER_RANK
+
+        def shrink_origin(o, carry):
+            def shrink_step(t, total):
+                k = pl.ds(pl.multiple_of(t * step, step), step)
+                x = rows[:, :, k].reshape(total_rows, step)
+                return total + jnp.dot(x, down[o, k, :], preferred_element_type=jnp.float32)
+
+            zero = jnp.zeros((total_rows, lanes), jnp.float32)
+            total = lax.fori_loop(0, width // step, shrink_step, zero)
+            kept = jnp.where(tag == o * (lanes // ADAPTER_RANK), total, 0.0)
+            shrink[o] = kept.astype(jnp.bfloat16)
+            return carry
+
+        lax.fori_loop(0, LINE, shrink_origin, 0)
+
+    def expand(t):
+        first, count = tiles[t]
         tile = 512
 
-        def up_step(t, carry):
-            c = pl.ds(pl.multiple_of(t * tile, tile), tile)
-            total = jnp.zeros((PLANE * count, tile), jnp.float32)
-            for m, o in zip(masked, origins):
-                total += jnp.dot(m, up[o, :, c], preferred_element_type=jnp.float32)
-            result[:, first : first + count, c] = total.astype(jnp.bfloat16).reshape(
-                PLANE, count, tile
-            )
+        def up_step(i, carry):
+            c = pl.ds(pl.multiple_of(first + i * tile, tile), tile)
+            total = jnp.zeros((total_rows, tile), jnp.float32)
+            for o in range(LINE):
+                total += jnp.dot(shrink[o], up[o, :, c], preferred_element_type=jnp.float32)
+            result[:, :, c] = total.astype(jnp.bfloat16).reshape(PLANE, slots, tile)
             return carry
 
-        lax.fori_loop(0, width // tile, up_step, 0)
+        lax.fori_loop(0, count // tile, up_step, 0)
         for e in range(1, PLANE):
-            back(phase, first, count, e, q).start()
-        keep_own(phase, first, count).start()
-
-    def arrive(origin):
-        for kind in range(2):
-            from_other(kind, origin).wait_recv()
-
-    near = z + 1 - 2 * (z % 2)
-    third = 2 - z // 2
-    far = 3 * (1 - z // 2)
-    phases = ((0, 2 * cap), (2 * cap, cap + 8), (3 * cap + 8, 2 * cap))
-
-    pass_on(1)
-    pass_on(2)
+            back(t, e, q).start()
+        keep_own(t).start()
+
+    for kind in range(DOWN_PARTS + 1):
+        pass_on(kind)
     for copy in own[2:]:
         copy.wait()
     for e in range(1, PLANE):
         tag_copy(e, (q + PLANE - e) % PLANE).wait_recv()
         token_copy(e, (q + PLANE - e) % PLANE).wait_recv()
-    arrive(near)
-    compute(0, *phases[0], (z, near))
-    pass_on(3)
-    arrive(third)
-    compute(1, *phases[1], (third,))
-    arrive(far)
-    compute(2, *phases[2], (z, near, third, far))
+    for kind in range(DOWN_PARTS):
+        arrive(kind)
+    shrink_all()
+    for t in range(len(tiles)):
+        if t + 1 < len(tiles):
+            pass_on(DOWN_PARTS + t + 1)
+        arrive(DOWN_PARTS + t)
+        expand(t)
 
     for e in range(1, PLANE):
         tag_copy(e, q).wait_send()
         token_copy(e, q).wait_send()
-    for kind in range(2):
+    for kind in range(kinds):
         for d in range(LINE):
             @pl.when((z >= d) & (z < LINE - 1))
             def _():
@@ -302,13 +311,13 @@
             def _():
                 to_left(kind, z + d).wait_send()
 
-        for origin in (near, third, far):
+        for origin in origins[1:]:
             to_other(kind, origin).wait_send()
-    for phase, (first, count) in enumerate(phases):
-        keep_own(phase, first, count).wait()
+    for t in range(len(tiles)):
+        keep_own(t).wait()
         for e in range(1, PLANE):
-            back(phase, first, count, e, q).wait_send()
-            back(phase, first, count, e, (q + PLANE - e) % PLANE).wait_recv()
+            back(t, e, q).wait_send()
+            back(t, e, (q + PLANE - e) % PLANE).wait_recv()
 
 
 def exchange_planes(
@@ -344,8 +353,11 @@
     tag = jnp.broadcast_to(tag.astype(jnp.bfloat16)[:, None], (PLANE * slots, lanes))
     tag = tag.reshape(PLANE, slots, lanes)
     dma = pltpu.SemaphoreType.DMA
+    eighth = width // 8
+    tiles = [(0, eighth), (eighth, eighth)] + [(i * eighth, 2 * eighth) for i in (2, 4, 6)]
+    kinds = DOWN_PARTS + len(tiles)
     returned = pl.pallas_call(
-        lambda *refs: plane_kernel(cap, *refs),
+        lambda *refs: plane_kernel(tiles, *refs),
         out_shape=jax.ShapeDtypeStruct((PLANE, slots, width), jnp.bfloat16),
         in_specs=[pl.BlockSpec(memory_space=pl.ANY)] * 4,
         out_specs=pl.BlockSpec(memory_space=pl.ANY),
@@ -355,19 +367,20 @@
             pltpu.VMEM((LINE, width, lanes), jnp.bfloat16),
             pltpu.VMEM((LINE, lanes, width), jnp.bfloat16),
             pltpu.VMEM((PLANE, slots, width), jnp.bfloat16),
+            pltpu.VMEM((LINE, PLANE * slots, lanes), jnp.bfloat16),
             dma((4,)),
             dma((PLANE,)),
             dma((PLANE,)),
             dma((PLANE,)),
             dma((PLANE,)),
-            dma((LINE, 2)),
-            dma((LINE, 2)),
-            dma((LINE, 2)),
-            dma((LINE, 2)),
-            dma((LINE, 2)),
-            dma((3, PLANE)),
-            dma((3, PLANE)),
-            dma((3,)),
+            dma((LINE, kinds)),
+            dma((LINE, kinds)),
+            dma((LINE, kinds)),
+            dma((LINE, kinds)),
+            dma((LINE, kinds)),
+            dma((len(tiles), PLANE)),
+            dma((len(tiles), PLANE)),
+            dma((len(tiles),)),
         ],
         compiler_params=pltpu.CompilerParams(
             collective_id=0, has_side_effects=True, vmem_limit_bytes=56 * 2**20

time: 235 us -> 239 us (1.017)
  the two profiles are of different devices: /device:TPU:17 before, /device:TPU:1 now
where the time goes in v2:
time: 239 us
  Pallas kernels  220 us (92%)
  matrix products  15.5 us (6%)
    pallas_call x1, Pallas kernels, exchange_planes(): pl.pallas_call(lambda *refs: plane_kernel(tiles, *refs), out_shape=jax.Sh...  220 us
    dot_general x1, matrix products, exchange_planes(): update = jnp.dot(pick.T, returned, preferred_element_type=jnp.float32)  7.8 us
    dot_general x1, matrix products, exchange_planes(): jnp.dot(pick, tokens, preferred_element_type=jnp.float32)  7.75 us

profile of v2, /device:TPU:1, one launch (start us, length us, event | category | flops | bytes accessed | tf_op | source)
XLA Modules:
  0.0 239.1 jit_solution(17182088019686175119)
XLA Ops:
  0.0 0.8 select_reduce_fusion.2
  0.9 0.8 copy.9
  1.6 0.1 reduce-window.8
  1.7 0.1 reduce
  1.8 0.7 sub.26
  2.4 0.1 select_reduce_fusion.1
  2.6 0.2 convert_reduce_fusion
  2.8 0.2 select_reduce_fusion
  2.9 0.8 broadcast_in_dim.78.refs_1_
  3.7 7.7 %convolution_convert_fusion = bf16[512,8192]{1,0:T(8,128)(2,1)} fusion(bf16[256,8192]{1,0:T(8,128)(2,1)} %param.6, s32[256]{0:T(256)S(1)} %fusion.6), kind=kOutput, calls=%fused_computation | convolution fusion | flops 2151809024 | bytes 12583936 | tf_op jit(solution)/shard_map/dot_general | solution.py:350
  11.5 219.8 %shard_map.64 = bf16[4,128,8192]{2,1,0:T(8,128)(2,1)} custom-call(bf16[4,128,8192]{2,1,0:T(8,128)(2,1)} %bitcast.7, bf16[4,128,128]{2,1,0:T(8,128)(2,1)} %broadcast_in_dim.78.refs_1_, bf16[8192,128]{1,0:T(8,128)(2,1)} %refs_2_.1, bf16[128,8192]{1,0:T(8,128)(2,1)} %refs_3_.1), custom_call_target="tpu_custom_call" | custom-call | flops 4294967296 | bytes 33554432 | tf_op jit(solution)/shard_map/pallas_call | solution.py:359
  231.3 7.8 %convolution_convert_fusion.1 = bf16[256,8192]{1,0:T(8,128)(2,1)} fusion(bf16[512,8192]{1,0:T(8,128)(2,1)} %bitcast.8, s32[256]{0:T(256)S(1)} %fusion.6), kind=kOutput, calls=%fused_computation.1 | convolution fusion | flops 2149711872 | bytes 12583936 | tf_op jit(solution)/shard_map/dot_general | solution.py:395
  (3 shorter events, 0.0 us)

commit v3 on v2

--- a/solution.py
+++ b/solution.py
@@ -85,14 +85,14 @@
 
 PLANE = 4
 LINE = 4
-DOWN_PARTS = 2
+DOWN_PARTS = 4
 MESH = pl.DeviceIdType.MESH
 
 
 def plane_kernel(
-    tiles, out_ref, tag_ref, down_ref, up_ref, ret_ref,
-    rows, tags, down, up, result, shrink,
-    local_sem, tok_send, tok_recv, tag_send, tag_recv,
+    tiles, tokens_ref, pick_ref, tag_ref, down_ref, up_ref, ret_ref,
+    stage, rows, tags, down, up, result, sums, shrink,
+    local_sem, tok_own, tok_send, tok_recv, tag_send, tag_recv,
     right_send, left_send, x_send, z_recv, x_recv, ret_send, ret_recv, own_sem,
 ):
     group = lax.axis_index("groups")
@@ -111,8 +111,7 @@
     own = [
         pltpu.make_async_copy(down_ref, down.at[z], local_sem.at[0]),
         pltpu.make_async_copy(up_ref, up.at[z], local_sem.at[1]),
-        pltpu.make_async_copy(out_ref.at[q], rows.at[q], local_sem.at[2]),
-        pltpu.make_async_copy(tag_ref.at[q], tags.at[q], local_sem.at[3]),
+        pltpu.make_async_copy(tag_ref.at[q], tags.at[q], local_sem.at[2]),
     ]
     for copy in own:
         copy.start()
@@ -178,11 +177,23 @@
     send_own(0)
     send_own(1)
 
-    def token_copy(e, slot):
+    step = half_down // DOWN_PARTS
+    slots = rows.shape[1]
+    lanes = down.shape[2]
+    total_rows = PLANE * slots
+
+    def token_copy(t, e, slot):
+        columns = pl.ds(t * step, step)
         return pltpu.make_async_remote_copy(
-            src_ref=out_ref.at[peer(e)], dst_ref=rows.at[slot],
-            send_sem=tok_send.at[e], recv_sem=tok_recv.at[e],
+            src_ref=stage.at[peer(e), :, columns], dst_ref=rows.at[slot, :, columns],
+            send_sem=tok_send.at[t, e], recv_sem=tok_recv.at[t, e],
             device_id=(group, z * PLANE + peer(e)), device_id_type=MESH,
+        )
+
+    def token_own(t):
+        columns = pl.ds(t * step, step)
+        return pltpu.make_async_copy(
+            stage.at[q, :, columns], rows.at[q, :, columns], tok_own.at[t]
         )
 
     def tag_copy(e, slot):
@@ -194,7 +205,22 @@
 
     for e in range(1, PLANE):
         tag_copy(e, q).start()
-        token_copy(e, q).start()
+
+    def send_tokens(t):
+        picked = jnp.dot(
+            pick_ref[...], tokens_ref[:, t * step : (t + 1) * step],
+            preferred_element_type=jnp.float32,
+        )
+        stage[:, :, t * step : (t + 1) * step] = picked.astype(jnp.bfloat16).reshape(
+            PLANE, slots, step
+        )
+        for e in range(1, PLANE):
+            token_copy(t, e, q).start()
+        token_own(t).start()
+
+    for part_at in range(DOWN_PARTS):
+        send_tokens(part_at)
+        send_tokens(part_at + DOWN_PARTS)
 
     def pass_on(kind):
         if kind + 2 < kinds:
@@ -237,33 +263,36 @@
             result.at[q, :, columns], ret_ref.at[q, :, columns], own_sem.at[t]
         )
 
-    slots = rows.shape[1]
-    lanes = down.shape[2]
-    total_rows = PLANE * slots
     origins = (z, z + 1 - 2 * (z % 2), 2 - z // 2, 3 * (1 - z // 2))
 
     def arrive(kind):
         for origin in origins[1:]:
             from_other(kind, origin).wait_recv()
 
-    def shrink_all():
-        step = 1024
+    def shrink_part(i):
+        arrive(i)
+        for t in (i, i + DOWN_PARTS):
+            token_own(t).wait()
+            for e in range(1, PLANE):
+                token_copy(t, e, (q + PLANE - e) % PLANE).wait_recv()
+
+        def shrink_origin(o, carry):
+            total = sums[o]
+            for t in (i, i + DOWN_PARTS):
+                k = slice(t * step, (t + 1) * step)
+                x = rows[:, :, k].reshape(total_rows, step)
+                total += jnp.dot(x, down[o, k, :], preferred_element_type=jnp.float32)
+            sums[o] = total
+            return carry
+
+        lax.fori_loop(0, LINE, shrink_origin, 0)
+
+    def mask_all():
         tag = tags[...].reshape(total_rows, lanes).astype(jnp.int32)
         tag = tag - lax.broadcasted_iota(jnp.int32, (total_rows, lanes), 1) // ADAPTER_RANK
-
-        def shrink_origin(o, carry):
-            def shrink_step(t, total):
-                k = pl.ds(pl.multiple_of(t * step, step), step)
-                x = rows[:, :, k].reshape(total_rows, step)
-                return total + jnp.dot(x, down[o, k, :], preferred_element_type=jnp.float32)
-
-            zero = jnp.zeros((total_rows, lanes), jnp.float32)
-            total = lax.fori_loop(0, width // step, shrink_step, zero)
-            kept = jnp.where(tag == o * (lanes // ADAPTER_RANK), total, 0.0)
+        for o in range(LINE):
+            kept = jnp.where(tag == o * (lanes // ADAPTER_RANK), sums[o], 0.0)
             shrink[o] = kept.astype(jnp.bfloat16)
-            return carry
-
-        lax.fori_loop(0, LINE, shrink_origin, 0)
 
     def expand(t):
         first, count = tiles[t]
@@ -282,16 +311,16 @@
             back(t, e, q).start()
         keep_own(t).start()
 
-    for kind in range(DOWN_PARTS + 1):
-        pass_on(kind)
+    sums[...] = jnp.zeros_like(sums)
+    pass_on(0)
+    for kind in range(DOWN_PARTS):
+        pass_on(kind + 1)
+        shrink_part(kind)
     for copy in own[2:]:
         copy.wait()
     for e in range(1, PLANE):
         tag_copy(e, (q + PLANE - e) % PLANE).wait_recv()
-        token_copy(e, (q + PLANE - e) % PLANE).wait_recv()
-    for kind in range(DOWN_PARTS):
-        arrive(kind)
-    shrink_all()
+    mask_all()
     for t in range(len(tiles)):
         if t + 1 < len(tiles):
             pass_on(DOWN_PARTS + t + 1)
@@ -300,7 +329,8 @@
 
     for e in range(1, PLANE):
         tag_copy(e, q).wait_send()
-        token_copy(e, q).wait_send()
+        for t in range(2 * DOWN_PARTS):
+            token_copy(t, e, q).wait_send()
     for kind in range(kinds):
         for d in range(LINE):
             @pl.when((z >= d) & (z < LINE - 1))
@@ -347,8 +377,6 @@
     slot_index = jnp.arange(PLANE * slots, dtype=jnp.int32)
     hit = slot_index[:, None] == slot_of_token[None, :]
     pick = hit.astype(jnp.bfloat16)
-    outgoing = jnp.dot(pick, tokens, preferred_element_type=jnp.float32).astype(jnp.bfloat16)
-    outgoing = outgoing.reshape(PLANE, slots, width)
     tag = jnp.sum(jnp.where(hit, (origin * loaded_block + block % loaded_block)[None, :], 0), axis=1)
     tag = jnp.broadcast_to(tag.astype(jnp.bfloat16)[:, None], (PLANE * slots, lanes))
     tag = tag.reshape(PLANE, slots, lanes)
@@ -359,18 +387,22 @@
     returned = pl.pallas_call(
         lambda *refs: plane_kernel(tiles, *refs),
         out_shape=jax.ShapeDtypeStruct((PLANE, slots, width), jnp.bfloat16),
-        in_specs=[pl.BlockSpec(memory_space=pl.ANY)] * 4,
+        in_specs=[pl.BlockSpec(memory_space=pltpu.VMEM)] * 2
+        + [pl.BlockSpec(memory_space=pl.ANY)] * 3,
         out_specs=pl.BlockSpec(memory_space=pl.ANY),
         scratch_shapes=[
+            pltpu.VMEM((PLANE, slots, width), jnp.bfloat16),
             pltpu.VMEM((PLANE, slots, width), jnp.bfloat16),
             pltpu.VMEM((PLANE, slots, lanes), jnp.bfloat16),
             pltpu.VMEM((LINE, width, lanes), jnp.bfloat16),
             pltpu.VMEM((LINE, lanes, width), jnp.bfloat16),
             pltpu.VMEM((PLANE, slots, width), jnp.bfloat16),
+            pltpu.VMEM((LINE, PLANE * slots, lanes), jnp.float32),
             pltpu.VMEM((LINE, PLANE * slots, lanes), jnp.bfloat16),
-            dma((4,)),
-            dma((PLANE,)),
-            dma((PLANE,)),
+            dma((3,)),
+            dma((2 * DOWN_PARTS,)),
+            dma((2 * DOWN_PARTS, PLANE)),
+            dma((2 * DOWN_PARTS, PLANE)),
             dma((PLANE,)),
             dma((PLANE,)),
             dma((LINE, kinds)),
@@ -390,7 +422,7 @@
             bytes_accessed=8 * PLANE * slots * width,
             transcendentals=0,
         ),
-    )(outgoing, tag, down_weight, up_weight)
+    )(tokens, pick, tag, down_weight, up_weight)
     returned = returned.reshape(PLANE * slots, width)
     update = jnp.dot(pick.T, returned, preferred_element_type=jnp.float32)
     return update.astype(jnp.bfloat16)

time: 239 us -> 225 us (0.941)
  Pallas kernels: 220 us -> 212 us
  matrix products: 15.5 us -> 7.8 us
    dot_general x1 -> x0, matrix products: 7.75 us -> none  [exchange_planes(): jnp.dot(pick, tokens, preferred_element_type=jnp.float32)]
    pallas_call x1, Pallas kernels: 220 us -> 212 us  [exchange_planes(): pl.pallas_call(lambda *refs: plane_kernel(tiles, *refs), out_shape=jax.Sh...]
where the time goes in v3:
time: 225 us; the launch traced here: 224 us
  Pallas kernels  212 us (94%)
  matrix products  7.8 us (3%)
  other arithmetic  2.92 us (1%)
    pallas_call x1, Pallas kernels, exchange_planes(): pl.pallas_call(lambda *refs: plane_kernel(tiles, *refs), out_shape=jax.Sh...  212 us
    dot_general x1, matrix products, exchange_planes(): update = jnp.dot(pick.T, returned, preferred_element_type=jnp.float32)  7.8 us

profile of v3, /device:TPU:1, one launch (start us, length us, event | category | flops | bytes accessed | tf_op | source)
XLA Modules:
  0.0 224.5 jit_solution(8340560103300257642)
XLA Ops:
  0.0 0.8 select_reduce_fusion.2
  0.9 0.8 copy.9
  1.6 0.1 reduce-window.8
  1.7 0.1 reduce
  1.8 0.7 sub.26
  2.4 0.1 select_reduce_fusion.1
  2.6 0.2 convert_reduce_fusion
  2.8 0.2 select_reduce_fusion
  2.9 0.8 broadcast_in_dim.78.refs_2_
  3.7 0.8 fusion.refs_1_
  4.5 212.2 %shard_map.64 = bf16[4,128,8192]{2,1,0:T(8,128)(2,1)} custom-call(bf16[256,8192]{1,0:T(8,128)(2,1)} %refs_0_.1, bf16[512,256]{1,0:T(8,128)(2,1)} %fusion.refs_1_, bf16[4,128,128]{2,1,0:T(8,128)(2,1)} %broadcast_in_dim.78.refs_2_, bf16[8192,128]{1,0:T(8,128)(2,1)} %refs_3_.1, bf16[128,8192]{1,0:T(8,128)(2,1)} %refs_4_.1), custom_call_target="tpu_custom_call" | custom-call | flops 4294967296 | bytes 33554432 | tf_op jit(solution)/shard_map/pallas_call | solution.py:387
  216.7 7.8 %convolution_convert_fusion = bf16[256,8192]{1,0:T(8,128)(2,1)} fusion(bf16[512,8192]{1,0:T(8,128)(2,1)} %bitcast.5, s32[256]{0:T(256)S(1)} %fusion.6), kind=kOutput, calls=%fused_computation | convolution fusion | flops 2149711872 | bytes 12583936 | tf_op jit(solution)/shard_map/dot_general | solution.py:427
  (3 shorter events, 0.0 us)
